TPU v7x, 256 devices: a whole 4x4x8 slice. The times are simulated.
256 devices in a mesh: lat: 32 (over y, z_hi, core), lon: 8 (over z_lo, x).
Axes of the slice: x: 4, y: 4, z: 8 (z_hi: 4, z_lo: 2; z = z_hi * 2 + z_lo), core: 2. Of those that a mesh axis runs over, the one named last changes fastest.
Arguments:
- grid: bfloat16 [16, 5120, 11264], P(None, 'lat', 'lon'), may hold values from -6 to 6
- cycle_points: int32 [5120], replicated, may hold values from 20 to 10256, as said below
- pair_slot: int32 [160], replicated, may hold values from 0 to 159, each once
- polys: bfloat16 [160, 321, 2560], P('lat'), may hold values from -6 to 6
Outputs:
- spectra: float32 [16, 160, 321, 2], P('lon', 'lat')
Inputs may be any that keep to these rules, and one draw needn't show every extreme that they name: cycle_points[l] equals cycle_points[5119 - l], is a multiple of 4 and is at least 20 + 4 * min(l, 5119 - l); the largest value is reached at the equator. `pair_slot`: each slot number appears once.
All inputs are finite; a program needn't handle non-finite values.
Results may differ from a plain program's by a relative error of at most 0.0023.
Values may be sent and summed in bfloat16 or wider, within the bound.
A program may use at most 192 MiB of HBM per device.

v0:
```python
import math

import jax
import jax.numpy as jnp
from jax import lax
from jax.sharding import PartitionSpec as P

NLAT = 5120
MW = 320
BLK = 128
NH = 2560
M0 = 2240
ROWS = 321


two_pi = 2.0 * math.pi


def phase_angle(index_table, counts_cube):
    return two_pi * index_table.astype(jnp.float32) / counts_cube.astype(jnp.float32)


def cycle_transform(values, cycle_counts, wave_numbers, first_block):
    block_width = values.shape[3]
    window = wave_numbers.shape[0]
    highest = lax.Precision.HIGHEST
    offsets = jnp.arange(block_width, dtype=jnp.int32)
    blocks = first_block + jnp.arange(values.shape[2], dtype=jnp.int32)
    counts_cube = cycle_counts[:, None, None]
    inner_index = wave_numbers[None, None, :] * offsets[None, :, None] % counts_cube
    inner_angle = phase_angle(inner_index, counts_cube)
    inner_table = jnp.concatenate([jnp.cos(inner_angle), jnp.sin(inner_angle)], axis=-1).astype(
        jnp.bfloat16
    )
    positions = blocks[:, None] * block_width + offsets[None, :]
    inside = positions[None, :, :] < counts_cube
    masked = jnp.where(inside[None], values, jnp.zeros_like(values))
    partial_sums = jnp.einsum(
        "frab,rbc->frac", masked, inner_table, preferred_element_type=jnp.float32
    )
    cos_sums = partial_sums[..., :window]
    sin_sums = partial_sums[..., window:]
    outer_index = wave_numbers[None, None, :] * (block_width * blocks)[None, :, None] % counts_cube
    outer_angle = phase_angle(outer_index, counts_cube)
    outer_cos = jnp.cos(outer_angle)
    outer_sin = jnp.sin(outer_angle)
    real_part = jnp.einsum("rak,frak->fkr", outer_cos, cos_sums, precision=highest) - jnp.einsum(
        "rak,frak->fkr", outer_sin, sin_sums, precision=highest
    )
    imag_part = -(
        jnp.einsum("rak,frak->fkr", outer_sin, cos_sums, precision=highest)
        + jnp.einsum("rak,frak->fkr", outer_cos, sin_sums, precision=highest)
    )
    resolved = 2 * wave_numbers[:, None] < cycle_counts[None, :]
    row_scale = jnp.where(resolved, 1.0 / cycle_counts[None, :].astype(jnp.float32), 0.0)
    return jnp.stack([real_part * row_scale, imag_part * row_scale], axis=2)


def transform_cycles(values, cycle_counts, wave_numbers, first_block):
    field_count, cycle_total, row_length = values.shape
    cycle_block = 32
    block_count = cycle_total // cycle_block
    shaped = values.reshape(field_count, block_count, cycle_block, row_length // BLK, BLK)
    shaped = jnp.moveaxis(shaped, 1, 0)
    blocked_counts = cycle_counts.reshape(block_count, cycle_block)

    def one_block(pieces):
        return cycle_transform(pieces[0], pieces[1], wave_numbers, first_block)

    result = lax.map(one_block, (shaped, blocked_counts))
    result = jnp.moveaxis(result, 0, 3)
    return result.reshape(field_count, 2 * wave_numbers.shape[0], cycle_total)


def legendre(gathered, polys, pair_slot, lat_index):
    field_count = gathered.shape[0]
    local_slots = polys.shape[0]
    shaped = gathered.reshape(field_count, local_slots, 2, 2, NLAT)
    north_rows = shaped[..., :NH]
    south_rows = jnp.flip(shaped[..., NH:], axis=-1)
    folded = jnp.stack([north_rows + south_rows, north_rows - south_rows], axis=4)
    products = jnp.einsum(
        "srh,fsmqah->fsrmqa", polys.astype(jnp.float32), folded, precision=lax.Precision.HIGHEST
    )
    local_pairs = lax.dynamic_slice_in_dim(pair_slot, lat_index * local_slots, local_slots)
    row_index = jnp.arange(ROWS, dtype=jnp.int32)[None, :]
    split_row = (MW - local_pairs)[:, None]
    in_first = row_index < split_row
    degree = jnp.where(in_first, row_index, row_index - split_row)
    even_rows = degree % 2 == 0
    member = jnp.where(in_first[None, :, :, None, None], products[:, :, :, 0], products[:, :, :, 1])
    return jnp.where(even_rows[None, :, :, None], member[..., 0], member[..., 1])


def body(grid, cycle_points, pair_slot, polys):
    lat_index = lax.axis_index("lat")
    lon_index = lax.axis_index("lon")
    local_cycles = grid.shape[1]
    cycle_counts = lax.dynamic_slice_in_dim(cycle_points, lat_index * local_cycles, local_cycles)
    pair_order = jnp.stack([pair_slot, MW - 1 - pair_slot], axis=1).reshape(-1)
    wave_numbers = M0 + pair_order
    first_block = lon_index * (grid.shape[2] // BLK)
    fourier = transform_cycles(grid, cycle_counts, wave_numbers, first_block)
    gathered = lax.all_to_all(fourier, "lat", split_axis=1, concat_axis=2, tiled=True)
    spectra = lax.psum_scatter(
        legendre(gathered, polys, pair_slot, lat_index), "lon", scatter_dimension=0, tiled=True
    )
    return spectra


def solution(mesh):
    in_specs = (P(None, "lat", "lon"), P(), P(), P("lat", None, None))
    out_specs = P("lon", "lat", None, None)
    return jax.shard_map(body, mesh=mesh, in_specs=in_specs, out_specs=out_specs, check_vma=False)
```

profile of v0, /device:TPU:1, one launch (start us, length us, event | category | flops | bytes accessed | tf_op | source)
XLA Modules:
  0.0 1061.6 jit_solution(5392559425194080006)
XLA Ops:
  6.5 0.8 dynamic_slice.15
  7.4 14.6 %reshape.264 = bf16[16,5,32,11,128]{4,3,2,1,0:T(8,128)(2,1)} reshape(bf16[16,160,1408]{2,1,0:T(8,128)(2,1)} %param.6) | data formatting | bytes 14417920 | tf_op jit(solution)/shard_map/reshape | solution.py:63
  22.0 15.2 %copy.22 = bf16[5,16,32,11,128]{4,1,3,2,0:T(8,128)(2,1)} copy(bf16[5,16,32,11,128]{4,3,2,0,1:T(8,128)(2,1)} %bitcast.116) | data formatting | bytes 14417920 | tf_op jit(solution)/shard_map/while | solution.py:70
  37.5 592.5 %while.10 = (s32[]{:T(128)}, f32[5,16,320,2,32]{2,4,3,1,0:T(8,128)}, s32[320]{0:T(512)S(1)}, s32[5,32]{1,0:T(8,128)S(1)}, s32[]{:T(128)}, /*index=5*/bf16[5,16,32,11,128]{4,1,3,2,0:T(8,128)(2,1)}, s32[]{:T(128)}) while((s32[]{:T(128)}, f32[5,16,320,2,32]{2,4,3,1,0:T(8,128)}, s32[320]{0:T(512)S(1)}, s32[5,32]{1,0:T(8,128)S(1)}, s32[]{:T(128)}, ...), condition=%wide.region_1.2_spmd, body=%wide.region_0.1_spmd.sunk | while | flops 965830016 | bytes 52551612 | solution.py:70
  56.2 82.9 %cosine_convert_fusion.2 = (bf16[32,128,320]{2,1,0:T(8,128)(2,1)S(1)}, bf16[32,128,320]{2,1,0:T(8,128)(2,1)S(1)}) fusion(f32[32]{0:T(128)S(1)} %convert_element_type.46, pred[32]{0:T(512)(128)(4,1)S(1)} %broadcast_compare_fusion.4, s32[32]{0:T(128)S(1)} %get-tuple-element.130, s32[128,320]{1,0:T(8,128)S(1)} %iota_multiply_fusion.2), kind=kLoop, calls=%fused_computation.15.clone.1 | loop fusion | flops 15728640 | bytes 5407008 | tf_op jit(solution)/shard_map/convert
  139.3 8.7 convolution_bitcast_fusion.2
  148.0 10.4 sine_bitcast_fusion.2
  158.4 8.6 multiply_reduce_fusion.5
  167.1 1.0 fusion.43
  168.1 1.3 fusion.44
  169.4 82.9 %cosine_convert_fusion.2 = (bf16[32,128,320]{2,1,0:T(8,128)(2,1)S(1)}, bf16[32,128,320]{2,1,0:T(8,128)(2,1)S(1)}) fusion(f32[32]{0:T(128)S(1)} %convert_element_type.46, pred[32]{0:T(512)(128)(4,1)S(1)} %broadcast_compare_fusion.4, s32[32]{0:T(128)S(1)} %get-tuple-element.130, s32[128,320]{1,0:T(8,128)S(1)} %iota_multiply_fusion.2), kind=kLoop, calls=%fused_computation.15.clone.1 | loop fusion | flops 15728640 | bytes 5407008 | tf_op jit(solution)/shard_map/convert
  252.4 8.7 convolution_bitcast_fusion.2
  261.2 10.4 sine_bitcast_fusion.2
  271.6 8.6 multiply_reduce_fusion.5
  280.3 1.0 fusion.43
  281.2 1.3 fusion.44
  282.6 82.9 %cosine_convert_fusion.2 = (bf16[32,128,320]{2,1,0:T(8,128)(2,1)S(1)}, bf16[32,128,320]{2,1,0:T(8,128)(2,1)S(1)}) fusion(f32[32]{0:T(128)S(1)} %convert_element_type.46, pred[32]{0:T(512)(128)(4,1)S(1)} %broadcast_compare_fusion.4, s32[32]{0:T(128)S(1)} %get-tuple-element.130, s32[128,320]{1,0:T(8,128)S(1)} %iota_multiply_fusion.2), kind=kLoop, calls=%fused_computation.15.clone.1 | loop fusion | flops 15728640 | bytes 5407008 | tf_op jit(solution)/shard_map/convert
  365.6 8.7 convolution_bitcast_fusion.2
  374.4 10.4 sine_bitcast_fusion.2
  384.8 8.6 multiply_reduce_fusion.5
  393.5 1.0 fusion.43
  394.4 1.3 fusion.44
  395.8 82.9 %cosine_convert_fusion.2 = (bf16[32,128,320]{2,1,0:T(8,128)(2,1)S(1)}, bf16[32,128,320]{2,1,0:T(8,128)(2,1)S(1)}) fusion(f32[32]{0:T(128)S(1)} %convert_element_type.46, pred[32]{0:T(512)(128)(4,1)S(1)} %broadcast_compare_fusion.4, s32[32]{0:T(128)S(1)} %get-tuple-element.130, s32[128,320]{1,0:T(8,128)S(1)} %iota_multiply_fusion.2), kind=kLoop, calls=%fused_computation.15.clone.1 | loop fusion | flops 15728640 | bytes 5407008 | tf_op jit(solution)/shard_map/convert
  478.8 8.7 convolution_bitcast_fusion.2
  487.6 10.4 sine_bitcast_fusion.2
  498.0 8.6 multiply_reduce_fusion.5
  506.7 1.0 fusion.43
  507.6 1.3 fusion.44
  509.0 82.9 %cosine_convert_fusion.2 = (bf16[32,128,320]{2,1,0:T(8,128)(2,1)S(1)}, bf16[32,128,320]{2,1,0:T(8,128)(2,1)S(1)}) fusion(f32[32]{0:T(128)S(1)} %convert_element_type.46, pred[32]{0:T(512)(128)(4,1)S(1)} %broadcast_compare_fusion.4, s32[32]{0:T(128)S(1)} %get-tuple-element.130, s32[128,320]{1,0:T(8,128)S(1)} %iota_multiply_fusion.2), kind=kLoop, calls=%fused_computation.15.clone.1 | loop fusion | flops 15728640 | bytes 5407008 | tf_op jit(solution)/shard_map/convert
  592.1 8.7 convolution_bitcast_fusion.2
  600.8 10.4 sine_bitcast_fusion.2
  611.2 8.6 multiply_reduce_fusion.5
  619.9 1.0 fusion.43
  620.8 1.3 fusion.44
  630.0 25.5 %copy.64 = f32[16,320,2,5,32]{4,3,0,2,1:T(8,128)} copy(f32[16,320,2,5,32]{1,4,2,0,3:T(8,128)} %bitcast.23) | data formatting | bytes 13107200 | tf_op jit(solution)/shard_map/reshape | solution.py:72
  655.5 28.0 %reshape.277 = f32[16,640,160]{2,0,1:T(8,128)} reshape(f32[16,320,2,5,32]{4,3,0,2,1:T(8,128)} %copy.64) | data formatting | bytes 13107200 | tf_op jit(solution)/shard_map/reshape | solution.py:72
  683.5 12.8 %all-to-all-start = ((f32[16,640,160]{2,0,1:T(8,128)}), f32[16,640,160]{2,0,1:T(8,128)}, u32[]{:S(2)}, u32[]{:S(2)}) async-start(f32[16,640,160]{2,0,1:T(8,128)} %reshape.277), calls=%async_computation | async-start | bytes 20971520 | tf_op jit(solution)/shard_map/all_to_all | solution.py:104
  696.5 231.2 %all-to-all-done = f32[16,640,160]{2,0,1:T(8,128)} async-done(((f32[16,640,160]{2,0,1:T(8,128)}), f32[16,640,160]{2,0,1:T(8,128)}, u32[]{:S(2)}, u32[]{:S(2)}) %all-to-all-start) | async-done | bytes 6553632 | tf_op jit(solution)/shard_map/all_to_all | solution.py:104
  927.7 16.4 %copy.25 = f32[16,20,32,160]{3,2,0,1:T(8,128)} copy(f32[16,20,32,160]{3,0,1,2:T(8,128)} %bitcast.25) | data formatting | bytes 13107200 | tf_op jit(solution)/shard_map/all_to_all | solution.py:104
  944.2 12.1 %reshape.266 = f32[16,5,2,2,5120]{4,0,3,2,1:T(8,128)} reshape(f32[16,20,32,160]{3,2,0,1:T(8,128)} %copy.25) | data formatting | bytes 13107200 | tf_op jit(solution)/shard_map/reshape | solution.py:78
  956.3 1.9 slice-done
  958.2 8.4 rev.4
  966.6 3.6 add_bitcast_fusion
  970.3 11.7 %fusion.30 = f32[16,5,321,2,2,2]{2,0,5,4,3,1:T(8,128)S(1)} fusion(bf16[5,321,2560]{2,1,0:T(8,128)(2,1)} %param.9, f32[16,5,2,2,1,2560]{5,0,4,3,2,1:T(8,128)S(1)} %get-tuple-element.77, f32[16,5,2,2,1,2560]{5,0,4,3,2,1:T(8,128)S(1)} %get-tuple-element.76), kind=kOutput, calls=%fused_computation.67 | convolution fusion | flops 6312755200 | bytes 15592960 | tf_op jit(solution)/shard_map/srh,fsmqah->fsrmqa/dot_general | solution.py:82
  982.0 0.7 fusion.36
  984.0 69.0 %all-reduce.3.cloned.1.call-done = f32[16,5,321,2]{2,0,3,1:T(8,128)} async-done(((f32[16,5,321,2]{2,0,3,1:T(8,128)}), f32[16,5,321,2]{2,0,3,1:T(8,128)}) %all-reduce.3.cloned.1.call-update) | async-done | bytes 205456
  1053.0 0.9 constant_dynamic-slice_fusion.1
  1053.9 0.6 copy.29
  (72 shorter events, 3.1 us)
Async XLA Ops:
  22.0 15.2 %copy-start = (s32[160]{0:T(256)S(1)}, s32[160]{0:T(256)}, u32[]{:S(2)}) copy-start(s32[160]{0:T(256)} %param.8) | copy-start | bytes 1924
  683.5 244.2 %all-to-all-start = ((f32[16,640,160]{2,0,1:T(8,128)}), f32[16,640,160]{2,0,1:T(8,128)}, u32[]{:S(2)}, u32[]{:S(2)}) async-start(f32[16,640,160]{2,0,1:T(8,128)} %reshape.277), calls=%async_computation | async-start | bytes 20971520 | tf_op jit(solution)/shard_map/all_to_all | solution.py:104
  696.3 356.7 %all-reduce.3.cloned.1.call-start = ((), (), s32[]{:S(2)}) async-start(), calls=%async_computation.1 | async-start | bytes 491520
  956.3 1.9 slice-start
  970.2 12.5 %copy-start.1 = (u32[256]{0:T(256)S(1)}, u32[256]{0:T(256)}, u32[]{:S(2)}) copy-start(u32[256]{0:T(256)} %constant.86) | copy-start | bytes 3076
Sparse Core Ops, SparseCore 0:
  982.9 70.0 all-reduce.2
where the time goes:
time: 1070 us; the launch traced here: 1060 us
  other arithmetic  527 us (49%)
  waiting for transfers between devices  300 us (28%)
  local copies, waits for them, and re-layouts  125 us (12%)
  matrix products  55.1 us (5%)
  loops' own time  26.9 us (3%)
  between operations  14.4 us (1%)
  starting transfers between devices  12.8 us (1%)
    another operation x5, other arithmetic  414 us
    all_to_all x1, waiting for transfers between devices, body(): lax.all_to_all(fourier, 'lat', split_axis=1, concat_axis=2, tiled=True)  231 us
    while x10, other arithmetic  94.8 us
    unnamed x2, waiting for transfers between devices  69 us
    reshape x2, local copies, waits for them, and re-layouts, transform_cycles(): return result.reshape(field_count, 2 * wave_numbers.shape[0], cycle_total)  53.5 us
    dot_general x5, matrix products, cycle_transform(): jnp.einsum('frab,rbc->frac', masked, inner_table, preferred_element_type=...  43.4 us
    another operation x1, loops' own time, transform_cycles(): result = lax.map(one_block, (shaped, blocked_counts))  26.9 us
  transfers between devices with their start and end apart: 2, of which 2 were waited for; matrix products, arithmetic and copies ran while one was open for 0% of the time, Pallas kernels for 0%

commit v1 on v0

v1 whole, which is shorter than its diff:
```python
import functools, math
import jax, jax.numpy as jnp
from jax import lax
from jax.experimental import pallas as pl
from jax.experimental.pallas import tpu as pltpu
from jax.sharding import PartitionSpec as P

MW = 320
M0 = 2240
ROWS = 321

LB = 16

def sincos_turn(u):
    w = u - jnp.floor(u + 0.5)
    x = w * math.pi
    y = x * x
    s = x * (1.0 + y * (-1/6 + y * (1/120 + y * (-1/5040 + y * (1/362880 + y * (-1/39916800 + y * (1/6227020800)))))))
    c = 1.0 + y * (-1/2 + y * (1/24 + y * (-1/720 + y * (1/40320 + y * (-1/3628800 + y * (1/479001600))))))
    return 1.0 - 2.0 * s * s, 2.0 * s * c

def fmod(x, c):
    q = jnp.floor(x / c)
    r = x - q * c
    r = jnp.where(r < 0, r + c, r)
    return jnp.where(r >= c, r - c, r)

def cmul(p, q):
    return (p[0] * q[0] - p[1] * q[1], p[0] * q[1] + p[1] * q[0])

def kernel(meta, cnt, ccol, mrow, grid, out, gf, SE, R2, OC, OS, WC, WS, ob):
    i = pl.program_id(0)
    first = meta[0]
    lane = lax.broadcasted_iota(jnp.int32, (8, 128), 1)
    cosl = (lane % 4) < 2
    for g in range(2):
        c = ccol[pl.ds(pl.multiple_of(i * LB + g * 8, 8), 8), :]
        for kt in range(3):
            m = jnp.broadcast_to(mrow[0:1, kt * 128:(kt + 1) * 128], (8, 128))
            r1 = fmod(m, c)
            e1 = sincos_turn(r1 / c)
            rp = fmod(r1 * 128.0, c)
            p1 = sincos_turn(rp / c)
            r0 = fmod(rp * (first // 128 + 5).astype(jnp.float32), c)
            w = sincos_turn(r0 / c)
            scale = jnp.where(2.0 * m < c, 1.0 / c, 0.0)
            WC[g, kt] = w[0] * scale
            if kt == 2:
                WS[g, kt] = jnp.where(cosl, w[1] * scale, -(w[1] * scale))
            else:
                WS[g, kt] = w[1] * scale
            pj = p1
            for j in range(1, 6):
                if j > 1:
                    pj = cmul(pj, p1)
                OC[g, kt, j - 1] = pj[0]
                OS[g, kt, j - 1] = pj[1]
            E = {0: (jnp.ones((8, 128), jnp.float32), jnp.zeros((8, 128), jnp.float32)), 1: e1}
            for b in range(2, 16):
                E[b] = cmul(E[b // 2], E[b - b // 2])
            R2[g, kt] = 2.0 * E[8][0]
            for b in range(16):
                if kt < 2:
                    SE[g, 2 * kt, b * 8:(b + 1) * 8, :] = E[b][0]
                    SE[g, 2 * kt + 1, b * 8:(b + 1) * 8, :] = E[b][1]
                else:
                    SE[g, 4, b * 8:(b + 1) * 8, :] = jnp.where(cosl, E[b][0], E[b][1])
    for f in range(16):
        for a in range(11):
            gf[a, f * LB:(f + 1) * LB, :] = grid[f, :, a * 128:(a + 1) * 128].astype(jnp.float32)

    lane16 = lax.broadcasted_iota(jnp.int32, (16, 128), 1)

    def row(ref, s):
        return jnp.broadcast_to(ref[pl.ds(s, 1), :], (8, 128))

    def table(g, s, t, kt):
        r2 = row(R2.at[g, kt], s)
        vs = [SE[g, t, pl.ds(s, 8, stride=8), :], SE[g, t, pl.ds(64 + s, 8, stride=8), :]]
        for b1 in range(2, 16):
            vs.append(r2 * vs[-1] - vs[-2])
        return jnp.concatenate(vs, axis=0).astype(jnp.bfloat16)

    def do_lat(l):
        g = l // 8
        s = l % 8
        lim = cnt[i * LB + l] - first
        rows = []
        for a in range(11):
            x = gf[a, pl.ds(l, 16, stride=LB), :]
            rows.append(jnp.where(lane16 < lim - 128 * a, x, 0.0).astype(jnp.bfloat16))
        lhs = jnp.concatenate(rows, axis=0)
        for kt in range(3):
            if kt < 2:
                tab = jnp.concatenate([table(g, s, 2 * kt, kt), table(g, s, 2 * kt + 1, kt)], axis=1)
            else:
                tab = table(g, s, 4, 2)
            y = jnp.dot(lhs, tab, preferred_element_type=jnp.float32)
            wc = row(WC.at[g, kt], s)
            ws = row(WS.at[g, kt], s)
            oc = [row(OC.at[g, kt, j], s) for j in range(5)]
            os = [row(OS.at[g, kt, j], s) for j in range(5)]
            for h in range(2):
                def blk(a, t):
                    return y[a * 16 + h * 8:a * 16 + h * 8 + 8, t * 128:(t + 1) * 128]
                if kt < 2:
                    re = blk(5, 0)
                    im = blk(5, 1)
                    for j in range(1, 6):
                        cp, cm = blk(5 + j, 0), blk(5 - j, 0)
                        sp, sm = blk(5 + j, 1), blk(5 - j, 1)
                        re = re + (oc[j - 1] * (cp + cm) - os[j - 1] * (sp - sm))
                        im = im + (os[j - 1] * (cp - cm) + oc[j - 1] * (sp + sm))
                    ob[2 * kt, pl.ds(h * 8 * LB + l, 8, stride=LB), :] = re * wc - im * ws
                    ob[2 * kt + 1, pl.ds(h * 8 * LB + l, 8, stride=LB), :] = -(im * wc + re * ws)
                else:
                    u = blk(5, 0)
                    v = jnp.zeros_like(u)
                    for j in range(1, 6):
                        p, q = blk(5 + j, 0), blk(5 - j, 0)
                        u = u + oc[j - 1] * (p + q)
                        v = v + os[j - 1] * (p - q)
                    v = jnp.where(cosl, pltpu.roll(v, 126, 1), pltpu.roll(v, 2, 1))
                    z = jnp.where(cosl, u - v, -(u + v))
                    zs = jnp.where(cosl, pltpu.roll(z, 126, 1), pltpu.roll(z, 2, 1))
                    ob[4, pl.ds(h * 8 * LB + l, 8, stride=LB), :] = z * wc + zs * ws

    UN = 8
    def step(n, carry):
        for u in range(UN):
            do_lat(n * UN + u)
        return carry
    lax.fori_loop(0, LB // UN, step, 0)
    for f in range(16):
        for t in range(5):
            out[f, :, t * 128:(t + 1) * 128] = ob[t, f * LB:(f + 1) * LB, :].astype(jnp.bfloat16)


def fourier_local(grid, counts, waves, first):
    L = grid.shape[1]
    ccol = jnp.broadcast_to(counts.astype(jnp.float32)[:, None], (L, 128))
    f32 = jnp.float32
    return pl.pallas_call(
        kernel,
        grid=(L // LB,),
        in_specs=[
            pl.BlockSpec(memory_space=pltpu.SMEM),
            pl.BlockSpec(memory_space=pltpu.SMEM),
            pl.BlockSpec(memory_space=pltpu.VMEM),
            pl.BlockSpec(memory_space=pltpu.VMEM),
            pl.BlockSpec((16, LB, 1408), lambda i: (0, i, 0)),
        ],
        out_specs=pl.BlockSpec((16, LB, 640), lambda i: (0, i, 0)),
        out_shape=jax.ShapeDtypeStruct((16, L, 640), jnp.bfloat16),
        scratch_shapes=[
            pltpu.VMEM((11, 16 * LB, 128), f32),
            pltpu.VMEM((2, 5, 128, 128), f32),
            pltpu.VMEM((2, 3, 8, 128), f32),
            pltpu.VMEM((2, 3, 5, 8, 128), f32),
            pltpu.VMEM((2, 3, 5, 8, 128), f32),
            pltpu.VMEM((2, 3, 8, 128), f32),
            pltpu.VMEM((2, 3, 8, 128), f32),
            pltpu.VMEM((5, 16 * LB, 128), f32),
        ],
        compiler_params=pltpu.CompilerParams(vmem_limit_bytes=48 * 2**20),
        name="fourier",
    )(first[None].astype(jnp.int32), counts, ccol, waves[None, :], grid)


def k_layout(order):
    main = order[:, :8].reshape(256)
    mix = jnp.concatenate([order[:, 8:], order[:, 8:]], axis=1).reshape(128)
    return jnp.concatenate([main, mix])

def leg_kernel(split, polys, x, out):
    s = pl.program_id(0)
    xs = x[0]
    hi = xs.astype(jnp.bfloat16)
    lo = (xs - hi.astype(jnp.float32)).astype(jnp.bfloat16)
    z = jnp.concatenate([hi, lo], axis=0)
    y = lax.dot_general(z, polys[0], (((1,), (1,)), ((), ())), preferred_element_type=jnp.float32)
    y = y[:16] + y[16:]
    r = lax.broadcasted_iota(jnp.int32, (4, 321), 1)
    sp = split[s]
    first = r < sp
    d = jnp.where(first, r, r - sp)
    even = d % 2 == 0
    out[0] = jnp.where(even, jnp.where(first, y[0:4], y[4:8]), jnp.where(first, y[8:12], y[12:16]))

def legendre(split, polys, x):
    return pl.pallas_call(
        leg_kernel, grid=(5,),
        in_specs=[pl.BlockSpec(memory_space=pltpu.SMEM), pl.BlockSpec((1, 321, 2560), lambda s: (s, 0, 0)), pl.BlockSpec((1, 16, 2560), lambda s: (s, 0, 0))],
        out_specs=pl.BlockSpec((1, 4, 321), lambda s: (s, 0, 0)),
        out_shape=jax.ShapeDtypeStruct((5, 4, 321), jnp.float32),
        compiler_params=pltpu.CompilerParams(vmem_limit_bytes=32 * 2**20),
        name="legendre",
    )(split, polys, x)


def body(grid, cycle_points, pair_slot, polys):
    lat_index = lax.axis_index("lat")
    lon_index = lax.axis_index("lon")
    lats = grid.shape[1]
    counts = lax.dynamic_slice_in_dim(cycle_points, lat_index * lats, lats)
    order = jnp.stack([pair_slot, MW - 1 - pair_slot], axis=1).reshape(32, 10)
    waves = (M0 + k_layout(order)).astype(jnp.float32)
    part = fourier_local(grid, counts, waves, lon_index * grid.shape[2])
    got = lax.all_to_all(part, "lon", split_axis=0, concat_axis=0, tiled=True)
    total = got.reshape(8, 2, lats, 640).astype(jnp.float32).sum(0)
    main = total[..., :512].reshape(2, lats, 2, 2, 16, 8)
    main = jnp.transpose(main, (2, 4, 5, 3, 0, 1)).reshape(32, 8, 2, 2, lats)
    mix = jnp.transpose(total[..., 512:].reshape(2, lats, 32, 2, 2), (2, 4, 3, 0, 1))
    sent = jnp.concatenate([main, mix], axis=1)
    held = lax.all_to_all(sent, "lat", split_axis=0, concat_axis=0, tiled=True)
    north = held[:16]
    south = held[16:][::-1, ..., ::-1]
    folded = jnp.stack([north + south, north - south])
    folded = folded.reshape(2, 16, 5, 2, 2, 2, lats)
    x = jnp.transpose(folded, (2, 0, 3, 4, 5, 1, 6)).reshape(5, 16, 16 * lats)
    local = lax.dynamic_slice_in_dim(pair_slot, lat_index * 5, 5)
    y = legendre(MW - local, polys, x).reshape(5, 2, 2, ROWS)
    return jnp.transpose(y, (2, 0, 3, 1))


def solution(mesh):
    in_specs = (P(None, "lat", "lon"), P(), P(), P("lat", None, None))
    out_specs = P("lon", "lat", None, None)
    return jax.shard_map(body, mesh=mesh, in_specs=in_specs, out_specs=out_specs, check_vma=False)
```

time: 1070 us -> 138 us (0.13)
  other arithmetic: 527 us -> 3.73 us
  waiting for transfers between devices: 300 us -> 33.9 us
  local copies, waits for them, and re-layouts: 125 us -> 9.52 us
  matrix products: 55.1 us -> 0 us
  blocking collectives: 0 us -> 44.5 us
  Pallas kernels: 0 us -> 32.4 us
  loops' own time: 26.9 us -> 0 us
  between operations: 14.4 us -> 0.19 us
    another operation x11 -> x1, other arithmetic: 423 us -> 0.69 us  [body(): order = jnp.stack([pair_slot, MW - 1 - pair_slot], axis=1).reshape(32, 10)]
    all_to_all x1, waiting for transfers between devices: 231 us -> 33.9 us  [body(): held = lax.all_to_all(sent, 'lat', split_axis=0, concat_axis=0, tiled=True)]
    while x10 -> x0, other arithmetic: 94.8 us -> none
    reshape x5, local copies, waits for them, and re-layouts: 80.3 us -> 1.75 us  [the longest x1 0.87 us: body(): x = jnp.transpose(folded, (2, 0, 3, 4, 5, 1, 6)).reshape(5, 16, 16 * lats)]
    unnamed x2 -> x0, waiting for transfers between devices: 69 us -> none
    dot_general x6 -> x0, matrix products: 55.1 us -> none  [the longest x5 43.4 us: cycle_transform(): jnp.einsum('frab,rbc->frac', masked, inner_table, preferred_element_type=...]
    all_to_all x0 -> x1, blocking collectives: none -> 44.5 us  [body(): got = lax.all_to_all(part, 'lon', split_axis=0, concat_axis=0, tiled=True)]
    pallas_call x0 -> x2, Pallas kernels: none -> 32.4 us  [the longest x1 28.7 us: fourier_local(): pl.pallas_call(kernel, grid=(L // LB,), in_specs=[pl.BlockSpec(memory_spa...]
  transfers between devices with their start and end apart: 2 -> 1, of which waited for: 2 -> 1; matrix products, arithmetic and copies ran while one was open for 0% -> 0% of each run, Pallas kernels for 0% -> 0%
where the time goes in v1:
time: 138 us; the launch traced here: 137 us
  blocking collectives  44.5 us (32%)
  waiting for transfers between devices  33.9 us (25%)
  Pallas kernels  32.4 us (23%)
  starting transfers between devices  13 us (9%)
  local copies, waits for them, and re-layouts  9.52 us (7%)
  other arithmetic  3.73 us (3%)
    all_to_all x1, blocking collectives, body(): got = lax.all_to_all(part, 'lon', split_axis=0, concat_axis=0, tiled=True)  44.5 us
    all_to_all x1, waiting for transfers between devices, body(): held = lax.all_to_all(sent, 'lat', split_axis=0, concat_axis=0, tiled=True)  33.9 us
    pallas_call x1, Pallas kernels, fourier_local(): pl.pallas_call(kernel, grid=(L // LB,), in_specs=[pl.BlockSpec(memory_spa...  28.7 us
    all_to_all x1, starting transfers between devices, body(): held = lax.all_to_all(sent, 'lat', split_axis=0, concat_axis=0, tiled=True)  13 us
    unnamed x6, local copies, waits for them, and re-layouts  3.98 us
    pallas_call x1, Pallas kernels, legendre(): pl.pallas_call(leg_kernel, grid=(5,), in_specs=[pl.BlockSpec(memory_space...  3.69 us
  transfers between devices with their start and end apart: 1, of which 1 were waited for; matrix products, arithmetic and copies ran while one was open for 0% of the time, Pallas kernels for 0%

profile of v1, /device:TPU:1, one launch (start us, length us, event | category | flops | bytes accessed | tf_op | source)
XLA Modules:
  0.0 137.2 jit_solution(6280017124130535873)
XLA Ops:
  0.0 0.7 broadcast_subtract_fusion
  0.7 0.7 pad_add_fusion.1
  1.4 0.1 copy.38
  1.5 0.1 reshape.63
  1.6 0.1 slice.26
  1.6 0.1 concatenate.21
  1.7 0.1 pad_add_fusion
  1.8 0.1 concatenate.23
  1.9 0.8 fusion.1
  2.7 0.1 broadcast_in_dim.5.ccol
  2.8 28.7 %fourier.1 = bf16[16,160,640]{2,1,0:T(8,128)(2,1)S(1)} custom-call(s32[1]{0:T(128)} %bitcast.meta, s32[160]{0:T(256)S(1)} %get-tuple-element.8.cnt, f32[160,128]{1,0:T(8,128)S(1)} %broadcast_in_dim.5.ccol, f32[1,384]{1,0:T(1,128)S(1)} %fusion.mrow, bf16[16,160,1408]{2,1,0:T(8,128)(2,1)} %grid.1), custom_call_target="tpu_custom_call" | custom-call | tf_op jit(solution)/shard_map/fourier/pallas_call | solution.py:143
  31.6 44.5 %all_to_all.10 = bf16[16,160,640]{2,1,0:T(8,128)(2,1)S(1)} all-to-all(bf16[16,160,640]{2,1,0:T(8,128)(2,1)S(1)} %fourier.1), channel_id=1, replica_groups=mesh['lat'=32,'lon'=8] {'lon'}, dimensions={0} | all-to-all | bytes 6553600 | tf_op jit(solution)/shard_map/all_to_all | solution.py:209
  76.1 0.5 convert_reduce_fusion
  76.5 0.1 slice.27
  76.6 0.2 copy.41
  76.8 0.1 copy.54
  76.9 0.3 copy.39
  77.3 0.1 copy.40
  77.4 0.2 pad_maximum_fusion
  77.6 2.1 %copy.43 = f32[32,10,2,2,160]{4,3,2,1,0:T(2,128)} copy(f32[32,10,2,2,160]{4,1,3,2,0:T(8,128)S(1)} %pad_maximum_fusion) | data formatting | bytes 1638400 | tf_op jit(solution)/shard_map/concatenate | solution.py:214
  79.7 0.0 copy-start.1
  79.7 13.0 %all-to-all-start.1 = ((f32[32,10,2,2,160]{4,3,2,1,0:T(2,128)}), f32[32,10,2,2,160]{4,3,2,1,0:T(2,128)S(1)}, u32[]{:S(2)}, u32[]{:S(2)}) async-start(f32[32,10,2,2,160]{4,3,2,1,0:T(2,128)} %copy.43), calls=%async_computation.1 | async-start | bytes 2621440 | tf_op jit(solution)/shard_map/all_to_all | solution.py:215
  92.7 0.0 copy-done.1
  92.7 0.1 dynamic-slice_subtract_fusion.split
  92.8 33.9 %all-to-all-done.1 = f32[32,10,2,2,160]{4,3,2,1,0:T(2,128)S(1)} async-done(((f32[32,10,2,2,160]{4,3,2,1,0:T(2,128)}), f32[32,10,2,2,160]{4,3,2,1,0:T(2,128)S(1)}, u32[]{:S(2)}, u32[]{:S(2)}) %all-to-all-start.1) | async-done | bytes 819232 | tf_op jit(solution)/shard_map/all_to_all | solution.py:215
  126.7 0.5 fusion.2
  127.1 0.2 copy.49
  127.3 0.4 reverse
  127.7 0.3 copy_add_fusion
  128.1 0.2 copy_subtract_fusion
  128.3 0.2 maximum_bitcast_fusion
  128.5 0.1 copy.46
  128.6 0.9 reshape.67.x
  129.5 0.0 copy-start
  129.5 3.4 %copy-done = bf16[5,321,2560]{2,1,0:T(8,128)(2,1)S(1)} copy-done((bf16[5,321,2560]{2,1,0:T(8,128)(2,1)S(1)}, bf16[5,321,2560]{2,1,0:T(8,128)(2,1)}, u32[]{:S(2)}) %copy-start) | copy-done | bytes 8217624
  132.9 3.7 %legendre.1 = f32[5,4,321]{2,1,0:T(4,128)S(1)} custom-call(s32[5]{0:T(128)S(1)} %dynamic-slice_subtract_fusion.split, bf16[5,321,2560]{2,1,0:T(8,128)(2,1)S(1)} %copy-done, f32[5,16,2560]{2,1,0:T(8,128)S(1)} %reshape.67.x), custom_call_target="tpu_custom_call" | custom-call | tf_op jit(solution)/shard_map/legendre/pallas_call | solution.py:191
  136.6 0.6 copy.55
  (3 shorter events, 0.1 us)
Async XLA Ops:
  79.7 13.0 %copy-start.1 = (s32[160]{0:T(256)S(1)}, s32[160]{0:T(256)}, u32[]{:S(2)}) copy-start(s32[160]{0:T(256)} %param.6) | copy-start | bytes 1924
  79.7 46.9 %all-to-all-start.1 = ((f32[32,10,2,2,160]{4,3,2,1,0:T(2,128)}), f32[32,10,2,2,160]{4,3,2,1,0:T(2,128)S(1)}, u32[]{:S(2)}, u32[]{:S(2)}) async-start(f32[32,10,2,2,160]{4,3,2,1,0:T(2,128)} %copy.43), calls=%async_computation.1 | async-start | bytes 2621440 | tf_op jit(solution)/shard_map/all_to_all | solution.py:215
  129.5 3.4 %copy-start = (bf16[5,321,2560]{2,1,0:T(8,128)(2,1)S(1)}, bf16[5,321,2560]{2,1,0:T(8,128)(2,1)}, u32[]{:S(2)}) copy-start(bf16[5,321,2560]{2,1,0:T(8,128)(2,1)} %polys.1) | copy-start | bytes 24652804

commit v2 on v1

v2 whole, which is shorter than its diff:
```python
import math

import jax
import jax.numpy as jnp
from jax import lax
from jax.experimental import pallas as pl
from jax.experimental.pallas import tpu as pltpu
from jax.sharding import PartitionSpec as P

MW = 320
M0 = 2240
ROWS = 321
LB = 16
NB = 10
UN = 8
NLATDEV = 32
SEG = 1408
BF = jnp.bfloat16
F32 = jnp.float32
MESH = pl.DeviceIdType.MESH


def sincos_turn(u):
    x = (u - jnp.floor(u + 0.5)) * math.pi
    y = x * x
    s = x * (1.0 + y * (-1 / 6 + y * (1 / 120 + y * (-1 / 5040 + y * (1 / 362880 + y * (-1 / 39916800 + y * (1 / 6227020800)))))))
    c = 1.0 + y * (-1 / 2 + y * (1 / 24 + y * (-1 / 720 + y * (1 / 40320 + y * (-1 / 3628800 + y * (1 / 479001600))))))
    return 1.0 - 2.0 * s * s, 2.0 * s * c


def fmod(x, c):
    r = x - jnp.floor(x / c) * c
    r = jnp.where(r < 0, r + c, r)
    return jnp.where(r >= c, r - c, r)


def cmul(p, q):
    return (p[0] * q[0] - p[1] * q[1], p[0] * q[1] + p[1] * q[0])


def kernel(cnt, pairs, prow, grid, polys, out,
           gin, gf, mrow, SE, R2, OC, OS, WC, WS, ob, SF, SB, RA, RB, KP, SZ, RZ, TR, S3, R3, XA, XM, PV,
           gsem, psem, sa_s, sa_r, sb_s, sb_r, sz_s, sz_r, s3_s, s3_r):
    lat = lax.axis_index("lat")
    lon = lax.axis_index("lon")
    x = lax.rem(lon, 4)
    z = lon // 4
    right = z * 4 + lax.rem(x + 1, 4)
    left = z * 4 + lax.rem(x + 3, 4)
    across = (1 - z) * 4 + x
    south = lat // 16

    barrier = pltpu.get_barrier_semaphore()
    for peer in (right, left, across):
        pl.semaphore_signal(barrier, inc=1, device_id=(lat, peer), device_id_type=MESH)

    def greet(d, carry):
        pl.semaphore_signal(barrier, inc=1, device_id=(lax.rem(lat + d, NLATDEV), lon), device_id_type=MESH)
        return carry

    def grid_copy(n):
        src = n + south * (NB - 1 - 2 * n)
        return pltpu.make_async_copy(
            grid.at[:, pl.ds(pl.multiple_of(src * LB, LB), LB), :], gin.at[n], gsem.at[n])

    def load(n, carry):
        grid_copy(n).start()
        return carry

    lax.fori_loop(0, NB, load, 0)
    lax.fori_loop(1, NLATDEV, greet, 0)
    polys_copy = pltpu.make_async_copy(polys, PV, psem)
    polys_copy.start()

    lane = lax.broadcasted_iota(jnp.int32, (8, 128), 1)
    sub = lax.broadcasted_iota(jnp.int32, (8, 128), 0)
    lane16 = lax.broadcasted_iota(jnp.int32, (16, 128), 1)
    cosl = (lane % 4) < 2
    first = lon * SEG
    base = jnp.where(south == 1, NLATDEV - 1 - lat, lat) * (LB * NB)

    col = lax.broadcasted_iota(jnp.int32, (160, 384), 1)
    slot_of = jnp.where(col < 256, 5 * (col // 8) + (col % 8) // 2, 5 * ((col - 256) // 4) + 4)
    pick_slot = jnp.where(slot_of == lax.broadcasted_iota(jnp.int32, (160, 384), 0), 1.0, 0.0).astype(BF)
    held_pair = jnp.dot(jnp.broadcast_to(prow[...].astype(F32), (8, 160)).astype(BF), pick_slot, preferred_element_type=F32)
    col8 = lax.broadcasted_iota(jnp.int32, (8, 384), 1)
    mrow[...] = M0 + jnp.where(col8 % 2 == 0, held_pair, MW - 1 - held_pair)

    def row(ref, s):
        return jnp.broadcast_to(ref[pl.ds(s, 1), :], (8, 128))

    def seeds(n):
        for g in range(2):
            c = jnp.zeros((8, 128), F32)
            for j in range(8):
                c = jnp.where(sub == j, cnt[base + n * LB + g * 8 + j].astype(F32), c)
            for kt in range(3):
                m = mrow[:, kt * 128:(kt + 1) * 128]
                r1 = fmod(m, c)
                e1 = sincos_turn(r1 / c)
                rp = fmod(r1 * 128.0, c)
                p1 = sincos_turn(rp / c)
                r0 = fmod(rp * (lon * 11 + 5).astype(F32), c)
                w = sincos_turn(r0 / c)
                scale = jnp.where(2.0 * m < c, 1.0 / c, 0.0)
                WC[g, kt] = w[0] * scale
                ws = w[1] * scale
                WS[g, kt] = jnp.where(cosl, ws, -ws) if kt == 2 else ws
                pj = p1
                for j in range(5):
                    if j:
                        pj = cmul(pj, p1)
                    OC[g, kt, j] = pj[0]
                    OS[g, kt, j] = pj[1]
                E = [(jnp.ones((8, 128), F32), jnp.zeros((8, 128), F32)), e1]
                for b in range(2, 16):
                    E.append(cmul(E[b // 2], E[b - b // 2]))
                R2[g, kt] = 2.0 * E[8][0]
                for b in range(16):
                    if kt < 2:
                        SE[g, 2 * kt, b * 8:(b + 1) * 8, :] = E[b][0]
                        SE[g, 2 * kt + 1, b * 8:(b + 1) * 8, :] = E[b][1]
                    else:
                        SE[g, 4, b * 8:(b + 1) * 8, :] = jnp.where(cosl, E[b][0], E[b][1])

    def table(g, s, t, kt):
        r2 = row(R2.at[g, kt], s)
        vs = [SE[g, t, pl.ds(s, 8, stride=8), :], SE[g, t, pl.ds(64 + s, 8, stride=8), :]]
        for _ in range(2, 16):
            vs.append(r2 * vs[-1] - vs[-2])
        return jnp.concatenate(vs, axis=0).astype(BF)

    def one_cycle(n, g, s):
        l = g * 8 + s
        lsrc = l + south * (LB - 1 - 2 * l)
        lim = cnt[base + n * LB + l] - first
        rows = []
        for a in range(11):
            v = gf[a, pl.ds(lsrc, 16, stride=LB), :]
            rows.append(jnp.where(lane16 < lim - 128 * a, v, 0.0).astype(BF))
        lhs = jnp.concatenate(rows, axis=0)
        for kt in range(3):
            if kt < 2:
                tab = jnp.concatenate([table(g, s, 2 * kt, kt), table(g, s, 2 * kt + 1, kt)], axis=1)
            else:
                tab = table(g, s, 4, 2)
            y = jnp.dot(lhs, tab, preferred_element_type=F32)
            wc = row(WC.at[g, kt], s)
            ws = row(WS.at[g, kt], s)
            oc = [row(OC.at[g, kt, j], s) for j in range(5)]
            os = [row(OS.at[g, kt, j], s) for j in range(5)]
            for h in range(2):
                def blk(a, t):
                    return y[a * 16 + h * 8:a * 16 + h * 8 + 8, t * 128:(t + 1) * 128]
                place = pl.ds(h * 8 * LB + l, 8, stride=LB)
                if kt < 2:
                    re = blk(5, 0)
                    im = blk(5, 1)
                    for j in range(1, 6):
                        cp, cm = blk(5 + j, 0), blk(5 - j, 0)
                        sp, sm = blk(5 + j, 1), blk(5 - j, 1)
                        re = re + (oc[j - 1] * (cp + cm) - os[j - 1] * (sp - sm))
                        im = im + (os[j - 1] * (cp - cm) + oc[j - 1] * (sp + sm))
                    ob[2 * kt, place, :] = re * wc - im * ws
                    ob[2 * kt + 1, place, :] = -(im * wc + re * ws)
                else:
                    u = blk(5, 0)
                    v = jnp.zeros_like(u)
                    for j in range(1, 6):
                        p, q = blk(5 + j, 0), blk(5 - j, 0)
                        u = u + oc[j - 1] * (p + q)
                        v = v + os[j - 1] * (p - q)
                    v = jnp.where(cosl, pltpu.roll(v, 126, 1), pltpu.roll(v, 2, 1))
                    w = jnp.where(cosl, u - v, -(u + v))
                    wsw = jnp.where(cosl, pltpu.roll(w, 126, 1), pltpu.roll(w, 2, 1))
                    ob[4, place, :] = w * wc + wsw * ws

    def remote(src, dst, ssem, rsem, la, lo):
        return pltpu.make_async_remote_copy(
            src_ref=src, dst_ref=dst, send_sem=ssem, recv_sem=rsem, device_id=(la, lo), device_id_type=MESH)

    def copy_a(n, side):
        return remote(SB.at[n, 2, side], RA.at[n, side], sa_s.at[n, side], sa_r.at[n, side], lat, (right, left)[side])

    def copy_b(n, side):
        return remote(SB.at[n, 1 + 2 * side], RB.at[n, side], sb_s.at[n, side], sb_r.at[n, side], lat, (right, left)[side])

    def copy_z(n):
        return remote(SZ.at[n], RZ.at[n], sz_s.at[n], sz_r.at[n], lat, across)

    LO, HI = (0, 8, 16, 24, 40, 48), (8, 16, 24, 40, 48, 56)

    def copy_3(c, d):
        to = lax.rem(lat + d, NLATDEV)
        return remote(S3.at[to, LO[c]:HI[c], :], R3.at[lat, LO[c]:HI[c], :], s3_s.at[c, d - 1], s3_r.at[c, d - 1], to, lon)

    def stage_f(n):
        grid_copy(n).wait()

        seeds(n)
        for f in range(16):
            for a in range(11):
                gf[a, f * LB:(f + 1) * LB, :] = gin[n, f, :, a * 128:(a + 1) * 128].astype(F32)

        def part(g, carry):
            for u in range(UN):
                one_cycle(n, g, u)
            return carry

        lax.fori_loop(0, LB // UN, part, 0)
        for f in range(16):
            h, xd, i = f // 8, (f % 8) // 2, f % 2
            rel = lax.rem(xd + 4 - x, 4)
            for t in range(5):
                v = ob[t, f * LB:(f + 1) * LB, :]
                SF[n, rel, h, i * LB:(i + 1) * LB, t * 128:(t + 1) * 128] = v
                SB[n, rel, h, i * LB:(i + 1) * LB, t * 128:(t + 1) * 128] = v.astype(BF)

        @pl.when(n == 0)
        def _():
            pl.semaphore_wait(barrier, NLATDEV - 1 + 3)

        for side in range(2):
            copy_a(n, side).start()

    def stage_b(n):
        for side in range(2):
            copy_a(n, side).wait_recv()
            SB[n, 1 + 2 * side, side] = (SF[n, 1 + 2 * side, side] + RA[n, side].astype(F32)).astype(BF)
            copy_b(n, side).start()

    def stage_c(n):
        for side in range(2):
            copy_b(n, side).wait_recv()

        def total(h):
            return SF[n, 0, h] + RB[n, 0, h].astype(F32) + RB[n, 1, h].astype(F32)

        SZ[n] = total(1 - z).astype(BF)
        copy_z(n).start()
        KP[n] = total(z)

    def turn(t):
        return jnp.transpose(TR[t]).reshape(16, 8, 128)

    def send_chunk(c):
        mix = turn(4)
        for half in range(2):
            re, im = turn(2 * half), turn(2 * half + 1)
            for j in range(16):
                i = half * 16 + j
                if c < 4:
                    S3[i, LO[c]:LO[c] + 8, :] = jnp.where(lane < 64, re[j], pltpu.roll(im[j], 64, 1))
                    v = pltpu.roll(mix[i // 2], 4, 0) if i % 2 != c // 2 else mix[i // 2]
                    if c % 2:
                        v = pltpu.roll(v, 64, 1)
                    if c:
                        v = jnp.where((sub // 4 == c // 2) & (lane // 64 == c % 2), v, S3[i, 32:40, :])
                    S3[i, 32:40, :] = v
                else:
                    v = pltpu.roll(mix[i // 2], 4, 0) if i % 2 else mix[i // 2]
                    S3[i, LO[c]:HI[c], :] = jnp.where(
                        lane < 32, re[j], jnp.where(lane < 64, pltpu.roll(im[j], 32, 1), pltpu.roll(v, 64, 1)))

        def go(d, carry):
            copy_3(c, d).start()
            return carry

        lax.fori_loop(1, NLATDEV, go, 0)
        R3[lat, LO[c]:HI[c], :] = S3[lat, LO[c]:HI[c], :]

    def stage_d(n):
        copy_z(n).wait_recv()
        width = jnp.where(n < 8, 2 * LB, LB)
        for i in range(2):
            start = pl.multiple_of(i * width + jnp.where(n < 8, lax.rem(n, 2), 0) * LB, LB)
            for t in range(5):
                TR[t, pl.ds(start, LB), :] = (
                    KP[n, i * LB:(i + 1) * LB, t * 128:(t + 1) * 128]
                    + RZ[n, i * LB:(i + 1) * LB, t * 128:(t + 1) * 128].astype(F32))
        for c, last in enumerate((1, 3, 5, 7, 8, 9)):
            @pl.when(n == last)
            def _():
                send_chunk(c)

    def step(n, carry):
        @pl.when(n < NB)
        def _():
            stage_f(n)

        @pl.when((n >= 1) & (n < NB + 1))
        def _():
            stage_b(n - 1)

        def run(stage, lag):
            def upto(k):
                return jnp.clip(k - lag + jnp.where(k >= NB, 1, 0), 0, NB)

            def one(k, carry):
                stage(k)
                return carry

            lax.fori_loop(upto(n - 1), upto(n), one, 0)

        run(stage_c, 2)
        run(stage_d, 3)
        return carry

    lax.fori_loop(0, NB + 3, step, 0)

    for c in range(6):
        def got(d, carry):
            copy_3(c, d).wait_recv()
            return carry

        lax.fori_loop(1, NLATDEV, got, 0)
    polys_copy.wait()

    def roll(v, k):
        return pltpu.roll(v, k % 128, 1) if k % 128 else v

    def quad(qd, carry):
        for sa in range(2):
            def held(i, r):
                a = R3[qd * 4 + i, r:r + 8, :]
                b = R3[NLATDEV - 1 - (qd * 4 + i), r:r + 8, :]
                return a + b if sa == 0 else a - b

            def piece(i, c, f, q, o):
                if c == 4:
                    k = q * 32 + f * 16
                    return jnp.where(lane < o + 16, roll(held(i, 40), o - k), roll(held(i, 48), o + 16 - k))
                if q < 2:
                    return roll(held(i, 8 * c), o - (q * 64 + f * 32))
                v = held(i, 32)
                v = pltpu.roll(v, 4, 0) if c // 2 else v
                return roll(v, o - ((c % 2) * 64 + f * 32))

            for f in range(2):
                for q in range(3):
                    for t in range(5):
                        v = None
                        for o in range(4):
                            i, c = divmod(4 * t + o, 5)
                            w = piece(i, c, f, q, 32 * o)
                            v = w if o == 0 else jnp.where(lane < 32 * o, v, w)
                        if q < 2:
                            r = ((sa * 2 + f) * 2 + q) * 8
                            XA[qd * 5 + t, r:r + 8, :] = v
                        else:
                            r = (sa * 2 + f) * 8
                            XM[qd * 5 + t, r:r + 8, :] = v
        return carry

    lax.fori_loop(0, 4, quad, 0)

    def parts(v):
        hi = v.astype(BF)
        return hi, (v - hi.astype(F32)).astype(BF)

    rr = lax.broadcasted_iota(jnp.int32, (1, ROWS), 1)
    for s in range(5):
        tiles = []
        for t in range(20):
            if s < 4:
                v = jnp.concatenate([XA[t, pl.ds(2 * s + k, 8, stride=8), :] for k in range(2)], axis=0)
            else:
                v = XM[t]
            tiles.append(jnp.concatenate(parts(v), axis=0))
        zz = jnp.concatenate(tiles, axis=1)
        y = lax.dot_general(zz, PV[s], (((1,), (1,)), ((), ())), preferred_element_type=F32)
        half = zz.shape[0] // 2
        y = y[:half] + y[half:]
        sp = MW - pairs[lat * 5 + s]
        in_first = rr < sp
        even = jnp.where(in_first, rr, rr - sp) % 2 == 0

        def pick(k, sa, f, q):
            j = (k * 8 + sa * 4 + f * 2 + q) if s < 4 else ((sa * 2 + f) * 8 + q * 2 + k)
            return y[j:j + 1]

        for f in range(2):
            for q in range(2):
                out[s, f * 2 + q:f * 2 + q + 1, :] = jnp.where(
                    even, jnp.where(in_first, pick(0, 0, f, q), pick(1, 0, f, q)),
                    jnp.where(in_first, pick(0, 1, f, q), pick(1, 1, f, q)))

    def sent(n, carry):
        for side in range(2):
            copy_a(n, side).wait_send()
            copy_b(n, side).wait_send()
        copy_z(n).wait_send()
        return carry

    lax.fori_loop(0, NB, sent, 0)
    for c in range(6):
        def gone(d, carry):
            copy_3(c, d).wait_send()
            return carry

        lax.fori_loop(1, NLATDEV, gone, 0)


def transform(grid, counts, pairs, polys):
    V = pltpu.VMEM
    dma = pltpu.SemaphoreType.DMA
    return pl.pallas_call(
        kernel,
        in_specs=[
            pl.BlockSpec(memory_space=pltpu.SMEM),
            pl.BlockSpec(memory_space=pltpu.SMEM),
            pl.BlockSpec(memory_space=pltpu.VMEM),
            pl.BlockSpec(memory_space=pl.ANY),
            pl.BlockSpec(memory_space=pl.ANY),
        ],
        out_specs=pl.BlockSpec(memory_space=pltpu.VMEM),
        out_shape=jax.ShapeDtypeStruct((5, 4, ROWS), F32),
        scratch_shapes=[
            V((NB, 16, LB, SEG), BF),
            V((11, 16 * LB, 128), F32),
            V((8, 384), F32),
            V((2, 5, 128, 128), F32),
            V((2, 3, 8, 128), F32),
            V((2, 3, 5, 8, 128), F32),
            V((2, 3, 5, 8, 128), F32),
            V((2, 3, 8, 128), F32),
            V((2, 3, 8, 128), F32),
            V((5, 16 * LB, 128), F32),
            V((NB, 4, 2, 2 * LB, 640), F32),
            V((NB, 4, 2, 2 * LB, 640), BF),
            V((NB, 2, 2 * LB, 640), BF),
            V((NB, 2, 2, 2 * LB, 640), BF),
            V((NB, 2 * LB, 640), F32),
            V((NB, 2 * LB, 640), BF),
            V((NB, 2 * LB, 640), BF),
            V((5, 128, 128), F32),
            V((NLATDEV, 56, 128), F32),
            V((NLATDEV, 56, 128), F32),
            V((20, 64, 128), F32),
            V((20, 32, 128), F32),
            V((5, ROWS, 2560), BF),
            dma((NB,)), dma(()),
            dma((NB, 2)), dma((NB, 2)), dma((NB, 2)), dma((NB, 2)), dma((NB,)), dma((NB,)),
            dma((6, NLATDEV - 1)), dma((6, NLATDEV - 1)),
        ],
        compiler_params=pltpu.CompilerParams(
            vmem_limit_bytes=56 * 2**20, collective_id=0, has_side_effects=True),
        name="transform",
    )(counts, pairs, pairs[None, :], grid, polys)


def body(grid, cycle_points, pair_slot, polys):
    y = transform(grid, cycle_points, pair_slot, polys).reshape(5, 2, 2, ROWS)
    return jnp.transpose(y, (1, 0, 3, 2))


def solution(mesh):
    in_specs = (P(None, "lat", "lon"), P(), P(), P("lat", None, None))
    out_specs = P("lon", "lat", None, None)
    return jax.shard_map(body, mesh=mesh, in_specs=in_specs, out_specs=out_specs, check_vma=False)
```

time: 138 us -> 77.3 us (0.56)
  blocking collectives: 44.5 us -> 0 us
  Pallas kernels: 32.4 us -> 75.6 us
  waiting for transfers between devices: 33.9 us -> 0 us
  starting transfers between devices: 13 us -> 0 us
  local copies, waits for them, and re-layouts: 9.52 us -> 1.4 us
  other arithmetic: 3.73 us -> 0 us
    all_to_all x1 -> x0, blocking collectives: 44.5 us -> none  [body(): got = lax.all_to_all(part, 'lon', split_axis=0, concat_axis=0, tiled=True)]
    pallas_call x2 -> x1, Pallas kernels: 32.4 us -> 75.6 us  [transform(): pl.pallas_call(kernel, in_specs=[pl.BlockSpec(memory_space=pltpu.SMEM), p...]
    all_to_all x1 -> x0, waiting for transfers between devices: 33.9 us -> none  [body(): held = lax.all_to_all(sent, 'lat', split_axis=0, concat_axis=0, tiled=True)]
    all_to_all x1 -> x0, starting transfers between devices: 13 us -> none  [body(): held = lax.all_to_all(sent, 'lat', split_axis=0, concat_axis=0, tiled=True)]
    unnamed x6 -> x0, local copies, waits for them, and re-layouts: 3.98 us -> none
    concatenate x3 -> x0, local copies, waits for them, and re-layouts: 2.3 us -> none  [the longest x1 2.1 us: body(): sent = jnp.concatenate([main, mix], axis=1)]
  transfers between devices with their start and end apart: 1 -> 0, of which waited for: 1 -> 0; matrix products, arithmetic and copies ran while one was open for 0% -> 0% of each run, Pallas kernels for 0% -> 0%
where the time goes in v2:
time: 77.3 us; the launch traced here: 77 us
  Pallas kernels  75.6 us (98%)
  local copies, waits for them, and re-layouts  1.4 us (2%)
    pallas_call x1, Pallas kernels, transform(): pl.pallas_call(kernel, in_specs=[pl.BlockSpec(memory_space=pltpu.SMEM), p...  75.6 us

profile of v2, /device:TPU:1, one launch (start us, length us, event | category | flops | bytes accessed | tf_op | source)
XLA Modules:
  0.0 77.0 jit_solution(1720656910997627952)
XLA Ops:
  0.0 75.6 %transform.1 = f32[5,4,321]{2,1,0:T(4,128)} custom-call(s32[5120]{0:T(1024)} %cnt.1, s32[160]{0:T(256)} %pairs.1, s32[1,160]{1,0:T(1,128)} %bitcast.4, bf16[16,160,1408]{2,1,0:T(8,128)(2,1)} %grid.1, bf16[5,321,2560]{2,1,0:T(8,128)(2,1)} %polys.1), custom_call_target="tpu_custom_call" | custom-call | tf_op jit(solution)/shard_map/transform/pallas_call | solution.py:407
  75.6 0.8 %reshape.3 = f32[5,2,2,321]{3,2,1,0:T(2,128)S(1)} reshape(f32[5,4,321]{2,1,0:T(4,128)} %transform.1) | data formatting | bytes 51360 | tf_op jit(solution)/shard_map/reshape | solution.py:453
  76.4 0.6 copy.7

commit v3 on v2

--- a/solution.py
+++ b/solution.py
@@ -18,6 +18,7 @@
 BF = jnp.bfloat16
 F32 = jnp.float32
 MESH = pl.DeviceIdType.MESH
+STEPS = 32000.0
 
 
 def sincos_turn(u):
@@ -39,7 +40,7 @@
 
 
 def kernel(cnt, pairs, prow, grid, polys, out,
-           gin, gf, mrow, SE, R2, OC, OS, WC, WS, ob, SF, SB, RA, RB, KP, SZ, RZ, TR, S3, R3, XA, XM, PV,
+           gin, gf, mrow, SE, R2, OC, OS, WC, WS, ob, SF, SB, RA, RB, KP, SZ, RZ, TR, MX, CD, S3, R3, RD, XA, XM, PV,
            gsem, psem, sa_s, sa_r, sb_s, sb_r, sz_s, sz_r, s3_s, s3_r):
     lat = lax.axis_index("lat")
     lon = lax.axis_index("lon")
@@ -180,19 +181,19 @@
             src_ref=src, dst_ref=dst, send_sem=ssem, recv_sem=rsem, device_id=(la, lo), device_id_type=MESH)
 
     def copy_a(n, side):
-        return remote(SB.at[n, 2, side], RA.at[n, side], sa_s.at[n, side], sa_r.at[n, side], lat, (right, left)[side])
+        return remote(SB.at[n, 2, side], RA.at[n, side], sa_s, sa_r.at[n, side], lat, (right, left)[side])
 
     def copy_b(n, side):
-        return remote(SB.at[n, 1 + 2 * side], RB.at[n, side], sb_s.at[n, side], sb_r.at[n, side], lat, (right, left)[side])
+        return remote(SB.at[n, 1 + 2 * side], RB.at[n, side], sb_s, sb_r.at[n, side], lat, (right, left)[side])
 
     def copy_z(n):
-        return remote(SZ.at[n], RZ.at[n], sz_s.at[n], sz_r.at[n], lat, across)
-
-    LO, HI = (0, 8, 16, 24, 40, 48), (8, 16, 24, 40, 48, 56)
+        return remote(SZ.at[n], RZ.at[n], sz_s, sz_r.at[n], lat, across)
+
+    LO, HI = (0, 16, 48), (16, 48, 64)
 
     def copy_3(c, d):
         to = lax.rem(lat + d, NLATDEV)
-        return remote(S3.at[to, LO[c]:HI[c], :], R3.at[lat, LO[c]:HI[c], :], s3_s.at[c, d - 1], s3_r.at[c, d - 1], to, lon)
+        return remote(S3.at[to, LO[c]:HI[c], :], R3.at[lat, LO[c]:HI[c], :], s3_s, s3_r.at[c // 2], to, lon)
 
     def stage_f(n):
         grid_copy(n).wait()
@@ -244,23 +245,32 @@
         return jnp.transpose(TR[t]).reshape(16, 8, 128)
 
     def send_chunk(c):
-        mix = turn(4)
-        for half in range(2):
-            re, im = turn(2 * half), turn(2 * half + 1)
-            for j in range(16):
-                i = half * 16 + j
-                if c < 4:
-                    S3[i, LO[c]:LO[c] + 8, :] = jnp.where(lane < 64, re[j], pltpu.roll(im[j], 64, 1))
-                    v = pltpu.roll(mix[i // 2], 4, 0) if i % 2 != c // 2 else mix[i // 2]
-                    if c % 2:
-                        v = pltpu.roll(v, 64, 1)
-                    if c:
-                        v = jnp.where((sub // 4 == c // 2) & (lane // 64 == c % 2), v, S3[i, 32:40, :])
-                    S3[i, 32:40, :] = v
-                else:
-                    v = pltpu.roll(mix[i // 2], 4, 0) if i % 2 else mix[i // 2]
-                    S3[i, LO[c]:HI[c], :] = jnp.where(
-                        lane < 32, re[j], jnp.where(lane < 64, pltpu.roll(im[j], 32, 1), pltpu.roll(v, 64, 1)))
+        ts = [turn(t) for t in range(5)]
+        top = jnp.zeros((8, 128), F32)
+        for v in ts:
+            top = jnp.maximum(top, jnp.max(jnp.abs(v), axis=0))
+        top = jnp.broadcast_to(jnp.max(top, axis=0, keepdims=True), (8, 128))
+        code = jnp.ceil(jnp.log2(jnp.maximum(top, 1e-30)) * 64.0)
+        inv = STEPS * jnp.exp2(code * (-1.0 / 64.0))
+        qs = [jnp.floor(v * inv + 0.5) for v in ts]
+
+        def put(i, r, upper, lower):
+            S3[i, r:r + 16, :] = jnp.concatenate([upper, lower], axis=0).astype(jnp.int32).astype(jnp.int16)
+
+        if c == 0:
+            MX[...] = qs[4]
+            CD[...] = code
+        for i in range(NLATDEV):
+            half, j = i // 16, i % 16
+            re, im = qs[2 * half][j], qs[2 * half + 1][j]
+            mix = pltpu.roll(qs[4][i // 2], 4, 0) if i % 2 != c % 2 else qs[4][i // 2]
+            if c < 2:
+                put(i, LO[c], re, im)
+            if c == 1:
+                mix0 = pltpu.roll(MX[i // 2], 4, 0) if i % 2 else MX[i // 2]
+                put(i, 32, jnp.where(sub < 4, mix0, mix), jnp.where(sub == 0, CD[...], code))
+            if c == 2:
+                put(i, 48, jnp.where(lane < 64, re, pltpu.roll(mix, 64, 1)), jnp.where(lane < 64, im, pltpu.roll(code, 64, 1)))
 
         def go(d, carry):
             copy_3(c, d).start()
@@ -271,14 +281,14 @@
 
     def stage_d(n):
         copy_z(n).wait_recv()
-        width = jnp.where(n < 8, 2 * LB, LB)
+        width = jnp.where(n < 8, 4 * LB, 2 * LB)
         for i in range(2):
-            start = pl.multiple_of(i * width + jnp.where(n < 8, lax.rem(n, 2), 0) * LB, LB)
+            start = pl.multiple_of(i * width + lax.rem(n, 4) * LB, LB)
             for t in range(5):
                 TR[t, pl.ds(start, LB), :] = (
                     KP[n, i * LB:(i + 1) * LB, t * 128:(t + 1) * 128]
                     + RZ[n, i * LB:(i + 1) * LB, t * 128:(t + 1) * 128].astype(F32))
-        for c, last in enumerate((1, 3, 5, 7, 8, 9)):
+        for c, last in enumerate((3, 7, 9)):
             @pl.when(n == last)
             def _():
                 send_chunk(c)
@@ -288,13 +298,13 @@
         def _():
             stage_f(n)
 
-        @pl.when((n >= 1) & (n < NB + 1))
+        @pl.when((n >= 1) & (n < NB))
         def _():
             stage_b(n - 1)
 
         def run(stage, lag):
             def upto(k):
-                return jnp.clip(k - lag + jnp.where(k >= NB, 1, 0), 0, NB)
+                return jnp.clip(k - lag, 0, NB)
 
             def one(k, carry):
                 stage(k)
@@ -304,55 +314,101 @@
 
         run(stage_c, 2)
         run(stage_d, 3)
-        return carry
-
-    lax.fori_loop(0, NB + 3, step, 0)
-
-    for c in range(6):
-        def got(d, carry):
-            copy_3(c, d).wait_recv()
-            return carry
-
-        lax.fori_loop(1, NLATDEV, got, 0)
+
+        @pl.when(n == NB)
+        def _():
+            stage_b(n - 1)
+
+        return carry
+
+    lax.fori_loop(0, NB + 4, step, 0)
+
+    def drained(ref, sem):
+        pltpu.make_async_copy(ref, ref, sem).wait()
+
+    drained(RA, sa_s)
+    drained(RB, sb_s)
+    drained(SZ, sz_s)
+    others = pl.ds(0, NLATDEV - 1)
+    drained(S3.at[others], s3_s)
     polys_copy.wait()
+    drained(R3.at[others, 0:48, :], s3_r.at[0])
 
     def roll(v, k):
         return pltpu.roll(v, k % 128, 1) if k % 128 else v
 
-    def quad(qd, carry):
+    def scale(v):
+        return jnp.exp2(v * (1.0 / 64.0)) * (1.0 / STEPS)
+
+    def take(i, r):
+        v = R3[i, r:r + 16, :].astype(jnp.int32).astype(F32)
+        return v[:8], v[8:]
+
+    def fold(i, r, sa):
+        a = RD[i, r:r + 8, :]
+        b = RD[NLATDEV - 1 - i, r:r + 8, :]
+        return a + b if sa == 0 else a - b
+
+    def rows_of(sa, f, q):
+        return (XA, ((sa * 2 + f) * 2 + q) * 8) if q < 2 else (XM, (sa * 2 + f) * 8)
+
+    def decode_main(i, carry):
+        mix, codes = take(i, 32)
+        s0 = scale(jnp.broadcast_to(codes[0:1], (8, 128)))
+        s1 = scale(jnp.broadcast_to(codes[1:2], (8, 128)))
+        for r, sc in ((0, s0), (16, s1)):
+            re, im = take(i, r)
+            RD[i, r:r + 8, :] = re * sc
+            RD[i, r + 8:r + 16, :] = im * sc
+        RD[i, 32:40, :] = mix * jnp.where(sub < 4, s0, s1)
+        return carry
+
+    def quad_main(qd, carry):
         for sa in range(2):
-            def held(i, r):
-                a = R3[qd * 4 + i, r:r + 8, :]
-                b = R3[NLATDEV - 1 - (qd * 4 + i), r:r + 8, :]
-                return a + b if sa == 0 else a - b
-
-            def piece(i, c, f, q, o):
-                if c == 4:
-                    k = q * 32 + f * 16
-                    return jnp.where(lane < o + 16, roll(held(i, 40), o - k), roll(held(i, 48), o + 16 - k))
-                if q < 2:
-                    return roll(held(i, 8 * c), o - (q * 64 + f * 32))
-                v = held(i, 32)
-                v = pltpu.roll(v, 4, 0) if c // 2 else v
-                return roll(v, o - ((c % 2) * 64 + f * 32))
-
             for f in range(2):
                 for q in range(3):
-                    for t in range(5):
-                        v = None
-                        for o in range(4):
-                            i, c = divmod(4 * t + o, 5)
-                            w = piece(i, c, f, q, 32 * o)
-                            v = w if o == 0 else jnp.where(lane < 32 * o, v, w)
+                    v = []
+                    for i in range(4):
                         if q < 2:
-                            r = ((sa * 2 + f) * 2 + q) * 8
-                            XA[qd * 5 + t, r:r + 8, :] = v
+                            c0, c1 = fold(qd * 4 + i, q * 8, sa), fold(qd * 4 + i, 16 + q * 8, sa)
                         else:
-                            r = (sa * 2 + f) * 8
-                            XM[qd * 5 + t, r:r + 8, :] = v
-        return carry
-
-    lax.fori_loop(0, 4, quad, 0)
+                            c0 = fold(qd * 4 + i, 32, sa)
+                            c1 = pltpu.roll(c0, 4, 0)
+                        w = jnp.where(lane < 64, c0, roll(c1, 64)) if f == 0 else jnp.where(lane < 64, roll(c0, 64), c1)
+                        v.append(roll(w, 32 * i))
+                    ref, r = rows_of(sa, f, q)
+                    ref[qd * 5, r:r + 8, :] = v[0]
+                    ref[qd * 5 + 1, r:r + 8, :] = v[1]
+                    ref[qd * 5 + 2, r:r + 8, :] = jnp.where(lane < 32, v[1], v[2])
+                    ref[qd * 5 + 3, r:r + 8, :] = jnp.where(lane < 64, v[2], v[3])
+                    ref[qd * 5 + 4, r:r + 8, :] = v[3]
+        return carry
+
+    lax.fori_loop(0, NLATDEV, decode_main, 0)
+    lax.fori_loop(0, 4, quad_main, 0)
+
+    drained(R3.at[others, 48:64, :], s3_r.at[1])
+
+    def decode_rest(i, carry):
+        upper, lower = take(i, 48)
+        s2 = scale(jnp.where(lane < 64, pltpu.roll(lower, 64, 1), lower))
+        RD[i, 40:48, :] = upper * s2
+        RD[i, 48:56, :] = lower * s2
+        return carry
+
+    def quad_rest(qd, carry):
+        for sa in range(2):
+            for i in range(4):
+                re, im = fold(qd * 4 + i, 40, sa), fold(qd * 4 + i, 48, sa)
+                for f in range(2):
+                    for q in range(3):
+                        w = roll((re, im, re)[q], 32 * i - 32 * f - (64 if q == 2 else 0))
+                        ref, r = rows_of(sa, f, q)
+                        ref[qd * 5 + i + 1, r:r + 8, :] = jnp.where(lane // 32 == i, w, ref[qd * 5 + i + 1, r:r + 8, :])
+        return carry
+
+    lax.fori_loop(0, NLATDEV, decode_rest, 0)
+    lax.fori_loop(0, 4, quad_rest, 0)
 
     def parts(v):
         hi = v.astype(BF)
@@ -384,21 +440,6 @@
                 out[s, f * 2 + q:f * 2 + q + 1, :] = jnp.where(
                     even, jnp.where(in_first, pick(0, 0, f, q), pick(1, 0, f, q)),
                     jnp.where(in_first, pick(0, 1, f, q), pick(1, 1, f, q)))
-
-    def sent(n, carry):
-        for side in range(2):
-            copy_a(n, side).wait_send()
-            copy_b(n, side).wait_send()
-        copy_z(n).wait_send()
-        return carry
-
-    lax.fori_loop(0, NB, sent, 0)
-    for c in range(6):
-        def gone(d, carry):
-            copy_3(c, d).wait_send()
-            return carry
-
-        lax.fori_loop(1, NLATDEV, gone, 0)
 
 
 def transform(grid, counts, pairs, polys):
@@ -434,14 +475,17 @@
             V((NB, 2 * LB, 640), BF),
             V((NB, 2 * LB, 640), BF),
             V((5, 128, 128), F32),
-            V((NLATDEV, 56, 128), F32),
+            V((16, 8, 128), F32),
+            V((8, 128), F32),
+            V((NLATDEV, 64, 128), jnp.int16),
+            V((NLATDEV, 64, 128), jnp.int16),
             V((NLATDEV, 56, 128), F32),
             V((20, 64, 128), F32),
             V((20, 32, 128), F32),
             V((5, ROWS, 2560), BF),
             dma((NB,)), dma(()),
-            dma((NB, 2)), dma((NB, 2)), dma((NB, 2)), dma((NB, 2)), dma((NB,)), dma((NB,)),
-            dma((6, NLATDEV - 1)), dma((6, NLATDEV - 1)),
+            dma(()), dma((NB, 2)), dma(()), dma((NB, 2)), dma(()), dma((NB,)),
+            dma(()), dma((2,)),
         ],
         compiler_params=pltpu.CompilerParams(
             vmem_limit_bytes=56 * 2**20, collective_id=0, has_side_effects=True),

time: 77.3 us -> 70.2 us (0.908)
  Pallas kernels: 75.6 us -> 68.5 us
    pallas_call x1, Pallas kernels: 75.6 us -> 68.5 us  [transform(): pl.pallas_call(kernel, in_specs=[pl.BlockSpec(memory_space=pltpu.SMEM), p...]
where the time goes in v3:
time: 70.2 us; the launch traced here: 69.9 us
  Pallas kernels  68.5 us (98%)
  local copies, waits for them, and re-layouts  1.4 us (2%)
    pallas_call x1, Pallas kernels, transform(): pl.pallas_call(kernel, in_specs=[pl.BlockSpec(memory_space=pltpu.SMEM), p...  68.5 us

profile of v3, /device:TPU:1, one launch (start us, length us, event | category | flops | bytes accessed | tf_op | source)
XLA Modules:
  0.0 69.9 jit_solution(11755645239746075291)
XLA Ops:
  0.0 68.5 %transform.1 = f32[5,4,321]{2,1,0:T(4,128)} custom-call(s32[5120]{0:T(1024)} %cnt.1, s32[160]{0:T(256)} %pairs.1, s32[1,160]{1,0:T(1,128)} %bitcast.4, bf16[16,160,1408]{2,1,0:T(8,128)(2,1)} %grid.1, bf16[5,321,2560]{2,1,0:T(8,128)(2,1)} %polys.1), custom_call_target="tpu_custom_call" | custom-call | tf_op jit(solution)/shard_map/transform/pallas_call | solution.py:448
  68.5 0.8 %reshape.3 = f32[5,2,2,321]{3,2,1,0:T(2,128)S(1)} reshape(f32[5,4,321]{2,1,0:T(4,128)} %transform.1) | data formatting | bytes 51360 | tf_op jit(solution)/shard_map/reshape | solution.py:497
  69.3 0.6 copy.7

commit v4 on v3

--- a/solution.py
+++ b/solution.py
@@ -11,6 +11,7 @@
 M0 = 2240
 ROWS = 321
 LB = 16
+GS = 24
 NB = 10
 UN = 8
 NLATDEV = 32
@@ -69,7 +70,7 @@
         return carry
 
     lax.fori_loop(0, NB, load, 0)
-    lax.fori_loop(1, NLATDEV, greet, 0)
+    lax.fori_loop(1, NLATDEV, greet, 0, unroll=True)
     polys_copy = pltpu.make_async_copy(polys, PV, psem)
     polys_copy.start()
 
@@ -137,7 +138,7 @@
         lim = cnt[base + n * LB + l] - first
         rows = []
         for a in range(11):
-            v = gf[a, pl.ds(lsrc, 16, stride=LB), :]
+            v = gf[a, pl.ds(lsrc, 16, stride=GS), :]
             rows.append(jnp.where(lane16 < lim - 128 * a, v, 0.0).astype(BF))
         lhs = jnp.concatenate(rows, axis=0)
         for kt in range(3):
@@ -153,7 +154,7 @@
             for h in range(2):
                 def blk(a, t):
                     return y[a * 16 + h * 8:a * 16 + h * 8 + 8, t * 128:(t + 1) * 128]
-                place = pl.ds(h * 8 * LB + l, 8, stride=LB)
+                place = pl.ds(h * 8 * GS + l, 8, stride=GS)
                 if kt < 2:
                     re = blk(5, 0)
                     im = blk(5, 1)
@@ -201,19 +202,20 @@
         seeds(n)
         for f in range(16):
             for a in range(11):
-                gf[a, f * LB:(f + 1) * LB, :] = gin[n, f, :, a * 128:(a + 1) * 128].astype(F32)
+                gf[a, f * GS:f * GS + LB, :] = gin[n, f, :, a * 128:(a + 1) * 128].astype(F32)
 
         def part(g, carry):
             for u in range(UN):
                 one_cycle(n, g, u)
             return carry
 
-        lax.fori_loop(0, LB // UN, part, 0)
+        for u in range(LB):
+            one_cycle(n, u // 8, u % 8)
         for f in range(16):
             h, xd, i = f // 8, (f % 8) // 2, f % 2
             rel = lax.rem(xd + 4 - x, 4)
             for t in range(5):
-                v = ob[t, f * LB:(f + 1) * LB, :]
+                v = ob[t, f * GS:f * GS + LB, :]
                 SF[n, rel, h, i * LB:(i + 1) * LB, t * 128:(t + 1) * 128] = v
                 SB[n, rel, h, i * LB:(i + 1) * LB, t * 128:(t + 1) * 128] = v.astype(BF)
 
@@ -276,7 +278,7 @@
             copy_3(c, d).start()
             return carry
 
-        lax.fori_loop(1, NLATDEV, go, 0)
+        lax.fori_loop(1, NLATDEV, go, 0, unroll=True)
         R3[lat, LO[c]:HI[c], :] = S3[lat, LO[c]:HI[c], :]
 
     def stage_d(n):
@@ -298,9 +300,9 @@
         def _():
             stage_f(n)
 
-        @pl.when((n >= 1) & (n < NB))
+        @pl.when((n >= 2) & (n < NB))
         def _():
-            stage_b(n - 1)
+            stage_b(n - 2)
 
         def run(stage, lag):
             def upto(k):
@@ -312,16 +314,17 @@
 
             lax.fori_loop(upto(n - 1), upto(n), one, 0)
 
-        run(stage_c, 2)
-        run(stage_d, 3)
+        run(stage_c, 3)
+        run(stage_d, 4)
 
         @pl.when(n == NB)
         def _():
+            stage_b(n - 2)
             stage_b(n - 1)
 
         return carry
 
-    lax.fori_loop(0, NB + 4, step, 0)
+    lax.fori_loop(0, NB + 5, step, 0)
 
     def drained(ref, sem):
         pltpu.make_async_copy(ref, ref, sem).wait()
@@ -437,7 +440,7 @@
 
         for f in range(2):
             for q in range(2):
-                out[s, f * 2 + q:f * 2 + q + 1, :] = jnp.where(
+                out[f, s, q:q + 1, :] = jnp.where(
                     even, jnp.where(in_first, pick(0, 0, f, q), pick(1, 0, f, q)),
                     jnp.where(in_first, pick(0, 1, f, q), pick(1, 1, f, q)))
 
@@ -455,10 +458,10 @@
             pl.BlockSpec(memory_space=pl.ANY),
         ],
         out_specs=pl.BlockSpec(memory_space=pltpu.VMEM),
-        out_shape=jax.ShapeDtypeStruct((5, 4, ROWS), F32),
+        out_shape=jax.ShapeDtypeStruct((2, 5, 2, ROWS), F32),
         scratch_shapes=[
             V((NB, 16, LB, SEG), BF),
-            V((11, 16 * LB, 128), F32),
+            V((11, 16 * GS, 128), F32),
             V((8, 384), F32),
             V((2, 5, 128, 128), F32),
             V((2, 3, 8, 128), F32),
@@ -466,7 +469,7 @@
             V((2, 3, 5, 8, 128), F32),
             V((2, 3, 8, 128), F32),
             V((2, 3, 8, 128), F32),
-            V((5, 16 * LB, 128), F32),
+            V((5, 16 * GS, 128), F32),
             V((NB, 4, 2, 2 * LB, 640), F32),
             V((NB, 4, 2, 2 * LB, 640), BF),
             V((NB, 2, 2 * LB, 640), BF),
@@ -494,8 +497,7 @@
 
 
 def body(grid, cycle_points, pair_slot, polys):
-    y = transform(grid, cycle_points, pair_slot, polys).reshape(5, 2, 2, ROWS)
-    return jnp.transpose(y, (1, 0, 3, 2))
+    return jnp.swapaxes(transform(grid, cycle_points, pair_slot, polys), 2, 3)
 
 
 def solution(mesh):

time: 70.2 us -> 66.8 us (0.952)
  Pallas kernels: 68.5 us -> 65.2 us
    pallas_call x1, Pallas kernels: 68.5 us -> 65.2 us  [transform(): pl.pallas_call(kernel, in_specs=[pl.BlockSpec(memory_space=pltpu.SMEM), p...]
    reshape x2 -> x0, local copies, waits for them, and re-layouts: 1.4 us -> none  [body(): y = transform(grid, cycle_points, pair_slot, polys).reshape(5, 2, 2, ROWS)]
    unnamed x0 -> x1, local copies, waits for them, and re-layouts: none -> 1.37 us
where the time goes in v4:
time: 66.8 us; the launch traced here: 66.6 us
  Pallas kernels  65.2 us (98%)
  local copies, waits for them, and re-layouts  1.37 us (2%)
    pallas_call x1, Pallas kernels, transform(): pl.pallas_call(kernel, in_specs=[pl.BlockSpec(memory_space=pltpu.SMEM), p...  65.2 us
    unnamed x1, local copies, waits for them, and re-layouts  1.37 us

profile of v4, /device:TPU:1, one launch (start us, length us, event | category | flops | bytes accessed | tf_op | source)
XLA Modules:
  0.0 66.6 jit_solution(18054895319626185189)
XLA Ops:
  0.0 65.2 %transform.1 = f32[2,5,2,321]{3,2,1,0:T(2,128)} custom-call(s32[5120]{0:T(1024)} %cnt.1, s32[160]{0:T(256)} %pairs.1, s32[1,160]{1,0:T(1,128)} %bitcast.3, bf16[16,160,1408]{2,1,0:T(8,128)(2,1)} %grid.1, bf16[5,321,2560]{2,1,0:T(8,128)(2,1)} %polys.1), custom_call_target="tpu_custom_call" | custom-call | tf_op jit(solution)/shard_map/transform/pallas_call | solution.py:451
  65.2 1.4 %copy.6 = f32[2,5,321,2]{2,3,1,0:T(2,128)} copy(f32[2,5,321,2]{2,3,1,0:T(2,128)} %bitcast.2) | data formatting | bytes 51360

commit v5 on v4

--- a/solution.py
+++ b/solution.py
@@ -300,31 +300,23 @@
         def _():
             stage_f(n)
 
-        @pl.when((n >= 2) & (n < NB))
+        @pl.when(n >= 2)
         def _():
             stage_b(n - 2)
 
         def run(stage, lag):
-            def upto(k):
-                return jnp.clip(k - lag, 0, NB)
-
             def one(k, carry):
                 stage(k)
                 return carry
 
-            lax.fori_loop(upto(n - 1), upto(n), one, 0)
-
-        run(stage_c, 3)
-        run(stage_d, 4)
-
-        @pl.when(n == NB)
-        def _():
-            stage_b(n - 2)
-            stage_b(n - 1)
-
-        return carry
-
-    lax.fori_loop(0, NB + 5, step, 0)
+            upto = jnp.where(n == NB + 1, NB, jnp.clip(n - lag + 1, 0, NB))
+            lax.fori_loop(jnp.clip(n - lag, 0, NB), upto, one, 0)
+
+        run(stage_c, 4)
+        run(stage_d, 5)
+        return carry
+
+    lax.fori_loop(0, NB + 2, step, 0)
 
     def drained(ref, sem):
         pltpu.make_async_copy(ref, ref, sem).wait()

time: 66.8 us -> 65.6 us (0.982)
  Pallas kernels: 65.2 us -> 64 us
    pallas_call x1, Pallas kernels: 65.2 us -> 64 us  [transform(): pl.pallas_call(kernel, in_specs=[pl.BlockSpec(memory_space=pltpu.SMEM), p...]
where the time goes in v5:
time: 65.6 us; the launch traced here: 65.4 us
  Pallas kernels  64 us (98%)
  local copies, waits for them, and re-layouts  1.37 us (2%)
    pallas_call x1, Pallas kernels, transform(): pl.pallas_call(kernel, in_specs=[pl.BlockSpec(memory_space=pltpu.SMEM), p...  64 us
    unnamed x1, local copies, waits for them, and re-layouts  1.37 us

profile of v5, /device:TPU:1, one launch (start us, length us, event | category | flops | bytes accessed | tf_op | source)
XLA Modules:
  0.0 65.4 jit_solution(11117312888075701011)
XLA Ops:
  0.0 64.0 %transform.1 = f32[2,5,2,321]{3,2,1,0:T(2,128)} custom-call(s32[5120]{0:T(1024)} %cnt.1, s32[160]{0:T(256)} %pairs.1, s32[1,160]{1,0:T(1,128)} %bitcast.3, bf16[16,160,1408]{2,1,0:T(8,128)(2,1)} %grid.1, bf16[5,321,2560]{2,1,0:T(8,128)(2,1)} %polys.1), custom_call_target="tpu_custom_call" | custom-call | tf_op jit(solution)/shard_map/transform/pallas_call | solution.py:443
  64.0 1.4 %copy.6 = f32[2,5,321,2]{2,3,1,0:T(2,128)} copy(f32[2,5,321,2]{2,3,1,0:T(2,128)} %bitcast.2) | data formatting | bytes 51360
